TPU v7x, 256 devices: a whole 4x4x8 slice. The times are simulated.
256 devices in a mesh: row: 16 (over z_lo, x, core), col: 16 (over z_hi, y).
Axes of the slice: x: 4, y: 4, z: 8 (z_hi: 4, z_lo: 2; z = z_hi * 2 + z_lo), core: 2. Of those that a mesh axis runs over, the one named last changes fastest.
Arguments:
- amplitudes: float32 [2048, 4096], P('row', 'col'), may hold values from -6 to 6
- integrals: float32 [4096, 32768], P('row', 'col'), may hold values from -0.25 to 0.25
- amp_mask: int32 [32, 64], replicated, may hold values from 0 to 1, as said below
- int_mask: int32 [64, 512], P('row', 'col'), may hold values from 0 to 1, as said below
- res_mask: int32 [32, 512], P(None, 'col'), may hold values from 0 to 1, as said below
Outputs:
- residual: float32 [2048, 32768], P('row', 'col')
Inputs may be any that keep to these rules, and one draw needn't show every extreme that they name: `amp_mask`: 1 marks a tile that is kept; any pattern of tiles may occur. `int_mask`: 1 marks a tile that is kept; any pattern of tiles may occur. `res_mask`: 1 marks a tile that is kept; any pattern of tiles may occur.
All inputs are finite; a program needn't handle non-finite values.
Results may differ from a plain program's by a relative error of at most 0.000076.
Values sent between devices are 32-bit elements; how exact they have to be, the bound alone decides.
A program may use at most 192 MiB of HBM per device.

v0:
```python
import jax
import jax.numpy as jnp
from jax import lax
from jax.sharding import PartitionSpec as P

TILE = 64


def spread(values, tiles):
    rows = tiles.shape[0]
    cols = tiles.shape[1]
    shaped = values.reshape(rows, TILE, cols, TILE)
    return (shaped * tiles.astype(jnp.float32)[:, None, :, None]).reshape(values.shape)


def row_tiles(tiles, first_row, count):
    tile_of_row = (first_row + lax.iota(jnp.int32, count)) // TILE
    onehot = (tile_of_row[:, None] == lax.iota(jnp.int32, tiles.shape[0])[None, :]).astype(
        jnp.float32
    )
    return jnp.dot(onehot, tiles.astype(jnp.float32), precision=lax.Precision.HIGHEST)


def mask_rows(values, selected):
    count = values.shape[0]
    blocks = selected.shape[1]
    shaped = values.reshape(count, blocks, TILE)
    return (shaped * selected[:, :, None]).reshape(values.shape)


def on_device(amplitudes, integrals, amp_mask, int_mask, res_mask):
    pair_rows = amplitudes.shape[0]
    position = lax.axis_index("row")
    first_pair = position * pair_rows
    full_cols = lax.all_gather(amplitudes, "col", axis=1, tiled=True)
    sparse_int = spread(integrals, int_mask)
    own_amp = mask_rows(full_cols, row_tiles(amp_mask, first_pair, pair_rows))
    product = jnp.dot(
        own_amp,
        lax.all_gather(sparse_int, "row", axis=0, tiled=True),
        preferred_element_type=jnp.float32,
        precision=lax.Precision.HIGHEST,
    )
    return mask_rows(product, row_tiles(res_mask, first_pair, pair_rows))


def solution(mesh):
    placed = (P("row", "col"), P("row", "col"), P(), P("row", "col"), P(None, "col"))
    return jax.shard_map(
        on_device, mesh=mesh, in_specs=placed, out_specs=P("row", "col"), check_vma=False
    )
```

profile of v0, /device:TPU:1, one launch (start us, length us, event | category | flops | bytes accessed | tf_op | source)
XLA Modules:
  0.0 316.2 jit_solution(16896108698530922170)
XLA Ops:
  6.5 0.0 all-gather.3.cloned.1.call-start
  6.5 1.7 copy.9
  8.2 0.0 all-gather.3.cloned.1.call-update
  8.2 0.0 all-gather.5.cloned.1.call-start
  8.3 0.7 convert_element_type.12
  9.0 2.5 mul.37
  11.5 3.6 %mul.38 = f32[256,2048]{1,0:T(8,128)S(1)} reshape(f32[4,64,32,64]{3,2,1,0:T(8,128)} %mul.37) | data formatting | bytes 4194304 | tf_op jit(solution)/shard_map/mul | solution.py:13
  15.1 3.2 %mul.39 = f32[256,2048]{1,0:T(8,128)} multiply(f32[256,2048]{1,0:T(8,128)} %param.6, f32[256,2048]{1,0:T(8,128)S(1)} %mul.38) | non-fusion elementwise | flops 524288 | bytes 6291456 | tf_op jit(solution)/shard_map/mul | solution.py:13
  18.3 0.0 copy-start
  18.3 0.0 copy-start.1
  18.3 0.0 all-gather.5.cloned.1.call-update
  18.4 0.7 copy-done
  19.0 0.2 fusion.5
  19.3 0.0 copy-done.1
  19.3 0.3 fusion.6
  19.6 53.2 %all-gather.3.cloned.1.call-done = f32[128,4096]{0,1:T(8,128)} async-done(((f32[128,256]{0,1:T(8,128)}), f32[128,4096]{0,1:T(8,128)}) %all-gather.3.cloned.1.call-update) | async-done | bytes 2097168 | tf_op jit(solution)/shard_map/all_gather | solution.py:35
  72.8 1.7 bitcast_multiply_fusion
  74.5 172.0 %all-gather.5.cloned.1.call-done = f32[4096,2048]{1,0:T(8,128)} async-done(((f32[256,2048]{1,0:T(8,128)}), f32[4096,2048]{1,0:T(8,128)}) %all-gather.5.cloned.1.call-update) | async-done | bytes 33554448 | tf_op jit(solution)/shard_map/all_gather | solution.py:40
  246.5 31.1 %copy.10 = f32[2048,4096]{1,0:T(8,128)} copy(f32[2048,4096]{0,1:T(8,128)} %bitcast.14) | data formatting | bytes 67108864 | tf_op jit(solution)/shard_map/dot_general | solution.py:38
  277.7 30.4 %fusion.2 = f32[128,32,64]{0,2,1:T(8,128)S(1)} fusion(f32[32,64,4096]{2,1,0:T(8,128)} %bitcast.13, f32[128,4096]{0,1:T(8,128)S(1)} %bitcast_multiply_fusion, f32[128,32]{0,1:T(8,128)S(1)} %fusion.5), kind=kOutput, calls=%fused_computation.3 | convolution fusion | flops 12885164032 | bytes 36716544 | tf_op jit(solution)/shard_map/dot_general | solution.py:38
  308.1 1.3 copy.12
  (1 shorter events, 0.0 us)
Async XLA Ops:
  6.5 66.2 %all-gather.3.cloned.1.call-start = ((), (), s32[]{:S(2)}) async-start(), calls=%async_computation | async-start | bytes 2228224 | tf_op jit(solution)/shard_map/all_gather | solution.py:35
  8.2 238.3 %all-gather.5.cloned.1.call-start = ((), (), s32[]{:S(2)}) async-start(), calls=%async_computation.1 | async-start | bytes 35651584 | tf_op jit(solution)/shard_map/all_gather | solution.py:40
  18.3 0.7 copy-start
  18.3 0.9 copy-start.1
Sparse Core Ops, SparseCore 0:
  9.8 62.9 all-gather.2
  74.6 171.8 all-gather.4
where the time goes:
time: 317 us; the launch traced here: 316 us
  waiting for transfers between devices  225 us (71%)
  local copies, waits for them, and re-layouts  40.9 us (13%)
  matrix products  30.9 us (10%)
  between operations  13.4 us (4%)
  other arithmetic  5.65 us (2%)
    all_gather x1, waiting for transfers between devices, on_device(): lax.all_gather(sparse_int, 'row', axis=0, tiled=True)  172 us
    all_gather x1, waiting for transfers between devices, on_device(): full_cols = lax.all_gather(amplitudes, 'col', axis=1, tiled=True)  53.2 us
    dot_general x1, local copies, waits for them, and re-layouts, on_device(): jnp.dot(own_amp, lax.all_gather(sparse_int, 'row', axis=0, tiled=True), p...  31.1 us
    dot_general x1, matrix products, on_device(): jnp.dot(own_amp, lax.all_gather(sparse_int, 'row', axis=0, tiled=True), p...  30.4 us
  transfers between devices with their start and end apart: 2, of which 2 were waited for; matrix products, arithmetic and copies ran while one was open for 4% of the time, Pallas kernels for 0%

commit v1 on v0

v1 whole, which is shorter than its diff:
```python
import jax
import jax.numpy as jnp
from jax import lax
from jax.experimental import pallas as pl
from jax.experimental.pallas import tpu as pltpu
from jax.sharding import PartitionSpec as P

TILE = 64
W = 256
HALF = 128
BACKLOG = 3
OWN, NEAR_Z, NEAR_X, FAR = 0, 1, 2, 3
MESH = pl.DeviceIdType.MESH
F32 = jnp.float32
BF16 = jnp.bfloat16


def device(x, z_lo, core, z_hi, y):
    return (z_lo * 8 + x * 2 + core, z_hi * 4 + y)


def remote(src, dst, send_sem, recv_sem, target):
    return pltpu.make_async_remote_copy(
        src_ref=src, dst_ref=dst, send_sem=send_sem, recv_sem=recv_sem,
        device_id=target, device_id_type=MESH,
    )


def onehot(shape, dim, offset):
    tile = lax.div(lax.broadcasted_iota(jnp.int32, shape, dim), TILE) + offset
    return (tile == lax.broadcasted_iota(jnp.int32, shape, 1 - dim)).astype(BF16)


def mm(a, b):
    return jnp.dot(a, b, preferred_element_type=F32)


def split(value):
    high = value.astype(BF16)
    return high, (value - high.astype(F32)).astype(BF16)


def kernel(
    amp_ref, int_ref, amp_mask_ref, int_mask_ref, res_mask_ref, out_ref,
    am, af, ah, al, bf, bh, bl, part, r1x, r1z, r2x, r2z, res_tiles, mask8,
    sa1, ra1, sa2, ra2, sb, rb, ss, rs, sf, rf, s1x, q1x, s1z, q1z, s2x, q2x, s2z, q2z,
):
    n = bf.shape[1]
    row, col = lax.axis_index("row"), lax.axis_index("col")
    core, x, z = lax.rem(row, 2), lax.rem(lax.div(row, 2), 4), lax.div(row, 8)
    y, h = lax.rem(col, 4), lax.div(col, 4)
    odd = lax.rem(x, 2)
    xa = x + 1 - 2 * odd
    xb = lax.rem(x + 3 + 2 * odd, 4)
    sib = device(x, z, 1 - core, h, y)
    dev_a = device(xa, z, core, h, y)
    dev_b = device(xb, z, core, h, y)
    dev_z = device(x, 1 - z, core, h, y)
    dev_y = [device(x, z, core, h, lax.rem(y + d, 4)) for d in (1, 2, 3)]
    kk = 2 * odd + core
    kk_sib = 2 * odd + 1 - core
    kk_a = 2 * (1 - odd) + core
    kk_as = 2 * (1 - odd) + 1 - core

    far_x = lax.rem(lax.rem(h, 2) + lax.div(x, 2), 2)
    to_x = x + far_x * (xb - x)
    to_z = lax.div(h, 2)
    far_z = lax.rem(to_z + z, 2)
    slot = 2 * far_x + far_z
    stays = slot == 0
    dev_h = [device(to_x, to_z, core, lax.rem(h + d, 4), y) for d in range(4)]
    from_h = 2 * z + lax.div(x, 2)
    sources = [
        (device(sx, sz, core, from_h, y), i)
        for i, (sx, sz) in enumerate(((x, z), (x, 1 - z), (xb, z), (xb, 1 - z)))
    ]
    hosts_self = from_h == h

    barrier = pltpu.get_barrier_semaphore()
    for peer in (sib, dev_a, dev_b, dev_z, *dev_y):
        pl.semaphore_signal(barrier, inc=1, device_id=peer, device_id_type=MESH)
    for peer, i in sources:
        if i == 0:
            @pl.when(jnp.logical_not(hosts_self))
            def _():
                pl.semaphore_signal(barrier, inc=1, device_id=peer, device_id_type=MESH)
        else:
            pl.semaphore_signal(barrier, inc=1, device_id=peer, device_id_type=MESH)

    rows = mm(onehot((2 * TILE, 32), 0, 2 * row), amp_mask_ref[...].astype(BF16)).astype(BF16)
    am[...] = amp_ref[...] * mm(rows, onehot((64, W), 1, 4 * col))
    mask8[...] = jnp.zeros_like(mask8)
    mask8[0:4, :] = int_mask_ref[...].astype(F32)

    pl.semaphore_wait(barrier, 11 - stays.astype(jnp.int32))

    def leg1(d):
        return remote(am, af.at[slot, y], sa1.at[d], ra1.at[slot], dev_h[d])

    @pl.when(stays)
    def _():
        pltpu.make_async_copy(am, af.at[slot, y], ra1.at[slot]).start()

    @pl.when(jnp.logical_not(stays))
    def _():
        leg1(0).start()

    for d in (1, 3, 2):
        leg1(d).start()

    def to_a(j):
        return remote(bf.at[kk, j], bf.at[kk, j], sb.at[j], rb.at[j], dev_a)

    def to_sib(j):
        return remote(bf.at[kk, j], bf.at[kk, j], ss.at[j], rs.at[j], sib)

    def forward(j):
        return remote(bf.at[kk_a, j], bf.at[kk_a, j], sf.at[j], rf.at[j], sib)

    mask8b = mask8[...].astype(BF16)
    for j in range(n):
        tiles = mm(mask8b, onehot((32, W), 1, (W // TILE) * j))
        for t in range(4):
            r = slice(t * TILE, (t + 1) * TILE)
            bf[kk, j, r, :] = int_ref[r, j * W:(j + 1) * W] * tiles[t:t + 1, :]
        to_a(j).start()
        to_sib(j).start()

    def leg2(s, d):
        return remote(af.at[s, y], af.at[s, y], sa2.at[s, d], ra2.at[s, d], dev_y[d])

    for s in (FAR, NEAR_X, NEAR_Z, OWN):
        remote(am, af.at[s, y], sa1.at[0], ra1.at[s], sib).wait_recv()
        for d in (0, 2, 1):
            leg2(s, d).start()

    res_rows = mm(onehot((2 * TILE, 32), 0, 2 * row), res_mask_ref[...].astype(BF16))
    res_tiles[...] = res_rows.astype(BF16)

    def take_amp(s):
        for d in range(3):
            leg2(s, d).wait_recv()
        for q in range(4):
            c = slice(q * W, (q + 1) * W)
            ah[s, :, c], al[s, :, c] = split(af[s, q])

    def take_int(j):
        remote(bf.at[kk_a, j], bf.at[kk_a, j], sb.at[j], rb.at[j], sib).wait_recv()
        forward(j).start()
        remote(bf.at[kk_sib, j], bf.at[kk_sib, j], ss.at[j], rs.at[j], sib).wait_recv()
        remote(bf.at[kk_as, j], bf.at[kk_as, j], sf.at[j], rf.at[j], sib).wait_recv()
        for q in range(4):
            r = slice(q * W, (q + 1) * W)
            bh[j, r, :], bl[j, r, :] = split(bf[q, j])

    def multiply(s, j):
        high = bh[j]
        total = mm(ah[s], high) + mm(al[s], high) + mm(ah[s], bl[j])
        part[s, j, 0] = total[:, :HALF]
        part[s, j, 1] = total[:, HALF:]

    def first_x(i, j):
        return remote(part.at[FAR - i, j, 0], r1x.at[j, i], s1x.at[j, i], q1x.at[j, i], dev_b)

    def first_z(i, j):
        s = FAR - 2 * i
        return remote(part.at[s, j, 1], r1z.at[j, i], s1z.at[j, i], q1z.at[j, i], dev_z)

    def second_z(j):
        return remote(part.at[NEAR_Z, j, 0], r2z.at[j], s2z.at[j], q2z.at[j], dev_z)

    def second_x(j):
        return remote(part.at[NEAR_X, j, 1], r2x.at[j], s2x.at[j], q2x.at[j], dev_b)

    def far(j):
        multiply(FAR, j)
        first_x(0, j).start()
        first_z(0, j).start()

    def near(j):
        multiply(NEAR_X, j)
        first_x(1, j).start()
        multiply(NEAR_Z, j)
        first_z(1, j).start()

    def second(j):
        first_x(0, j).wait_recv()
        part[NEAR_Z, j, 0] += r1x[j, 0]
        second_z(j).start()
        first_z(0, j).wait_recv()
        part[NEAR_X, j, 1] += r1z[j, 0]
        second_x(j).start()

    def loop(lo, hi, *steps):
        def body(j, carry):
            for step in steps:
                step(j)
            return carry

        lax.fori_loop(lo, hi, body, 0)

    take_amp(FAR)
    loop(0, BACKLOG, take_int, far)
    take_amp(NEAR_X)
    take_amp(NEAR_Z)
    loop(0, BACKLOG, near)
    loop(BACKLOG, n, take_int, far, near, lambda j: second(j - BACKLOG))
    take_amp(OWN)
    loop(0, n - BACKLOG, lambda j: multiply(OWN, j))
    loop(n - BACKLOG, n, second, lambda j: multiply(OWN, j))

    def finish(j):
        tiles = mm(res_tiles[...], onehot((32, W), 1, (W // TILE) * j))
        first_x(1, j).wait_recv()
        second_z(j).wait_recv()
        first_z(1, j).wait_recv()
        second_x(j).wait_recv()
        c = pl.multiple_of(j * W, W)
        left = part[OWN, j, 0] + r1x[j, 1] + r2z[j]
        right = part[OWN, j, 1] + r1z[j, 1] + r2x[j]
        out_ref[:, pl.ds(c, HALF)] = left * tiles[:, :HALF]
        out_ref[:, pl.ds(c + HALF, HALF)] = right * tiles[:, HALF:]

    loop(0, n, finish)

    @pl.when(jnp.logical_not(stays))
    def _():
        leg1(0).wait_send()

    for d in (1, 2, 3):
        leg1(d).wait_send()
    for s in range(4):
        for d in range(3):
            leg2(s, d).wait_send()

    def drain(j):
        to_a(j).wait_send()
        to_sib(j).wait_send()
        forward(j).wait_send()
        for i in range(2):
            first_x(i, j).wait_send()
            first_z(i, j).wait_send()
        second_x(j).wait_send()
        second_z(j).wait_send()

    loop(0, n, drain)


def on_device(amplitudes, integrals, amp_mask, int_mask, res_mask):
    rows, depth = amplitudes.shape
    cols = integrals.shape[1]
    n = cols // W
    dma = pltpu.SemaphoreType.DMA
    vmem = pltpu.VMEM
    return pl.pallas_call(
        kernel,
        out_shape=jax.ShapeDtypeStruct((rows, cols), F32),
        in_specs=[pl.BlockSpec(memory_space=pltpu.VMEM)] * 5,
        out_specs=pl.BlockSpec(memory_space=pltpu.VMEM),
        scratch_shapes=[
            vmem((rows, depth), F32),
            vmem((4, 4, rows, depth), F32),
            vmem((4, rows, 4 * depth), BF16),
            vmem((4, rows, 4 * depth), BF16),
            vmem((4, n, depth, W), F32),
            vmem((n, 4 * depth, W), BF16),
            vmem((n, 4 * depth, W), BF16),
            vmem((4, n, 2, rows, HALF), F32),
            vmem((n, 2, rows, HALF), F32),
            vmem((n, 2, rows, HALF), F32),
            vmem((n, rows, HALF), F32),
            vmem((n, rows, HALF), F32),
            vmem((rows, 32), BF16),
            vmem((8, 32), F32),
            dma((4,)), dma((4,)), dma((4, 3)), dma((4, 3)),
            dma((n,)), dma((n,)), dma((n,)), dma((n,)), dma((n,)), dma((n,)),
            dma((n, 2)), dma((n, 2)), dma((n, 2)), dma((n, 2)),
            dma((n,)), dma((n,)), dma((n,)), dma((n,)),
        ],
        compiler_params=pltpu.CompilerParams(
            collective_id=0, has_side_effects=True, vmem_limit_bytes=48 * 2**20
        ),
        cost_estimate=pl.CostEstimate(
            flops=2 * 3 * 4 * rows * 4 * depth * cols,
            bytes_accessed=4 * (rows * depth + depth * cols + rows * cols),
            transcendentals=0,
        ),
        name="ladder",
    )(amplitudes, integrals, amp_mask, int_mask, res_mask)


def solution(mesh):
    placed = (P("row", "col"), P("row", "col"), P(), P("row", "col"), P(None, "col"))
    return jax.shard_map(
        on_device, mesh=mesh, in_specs=placed, out_specs=P("row", "col"), check_vma=False
    )
```

time: 317 us -> 90.1 us (0.28)
  waiting for transfers between devices: 225 us -> 0 us
  Pallas kernels: 0 us -> 84.2 us
  local copies, waits for them, and re-layouts: 40.9 us -> 5.58 us
  matrix products: 30.9 us -> 0 us
  between operations: 13.4 us -> 0.01 us
  other arithmetic: 5.65 us -> 0 us
    all_gather x2 -> x0, waiting for transfers between devices: 225 us -> none  [the longest x1 172 us: on_device(): lax.all_gather(sparse_int, 'row', axis=0, tiled=True)]
    pallas_call x0 -> x1, Pallas kernels: none -> 84.2 us  [on_device(): pl.pallas_call(kernel, out_shape=jax.ShapeDtypeStruct((rows, cols), F32),...]
    dot_general x1 -> x0, local copies, waits for them, and re-layouts: 31.1 us -> none  [on_device(): jnp.dot(own_amp, lax.all_gather(sparse_int, 'row', axis=0, tiled=True), p...]
    dot_general x3 -> x0, matrix products: 30.9 us -> none  [the longest x1 30.4 us: on_device(): jnp.dot(own_amp, lax.all_gather(sparse_int, 'row', axis=0, tiled=True), p...]
    mul x2 -> x0, local copies, waits for them, and re-layouts: 6.14 us -> none  [spread(): shaped * tiles.astype(jnp.float32)[:, None, :, None]]
    mul x2 -> x0, other arithmetic: 4.96 us -> none  [the longest x1 3.22 us: spread(): shaped * tiles.astype(jnp.float32)[:, None, :, None]]
    unnamed x5 -> x11, local copies, waits for them, and re-layouts: 2.35 us -> 5.58 us
  transfers between devices with their start and end apart: 2 -> 0, of which waited for: 2 -> 0; matrix products, arithmetic and copies ran while one was open for 4% -> 0% of each run, Pallas kernels for 0% -> 0%
where the time goes in v1:
time: 90.1 us; the launch traced here: 89.8 us
  Pallas kernels  84.2 us (93%)
  local copies, waits for them, and re-layouts  5.58 us (6%)
    pallas_call x1, Pallas kernels, on_device(): pl.pallas_call(kernel, out_shape=jax.ShapeDtypeStruct((rows, cols), F32),...  84.2 us
    unnamed x11, local copies, waits for them, and re-layouts  5.58 us

profile of v1, /device:TPU:1, one launch (start us, length us, event | category | flops | bytes accessed | tf_op | source)
XLA Modules:
  0.0 89.8 jit_solution(7262446164030288990)
XLA Ops:
  0.0 0.0 copy-start
  0.0 1.6 %copy-done = f32[256,2048]{1,0:T(8,128)S(1)} copy-done((f32[256,2048]{1,0:T(8,128)S(1)}, f32[256,2048]{1,0:T(8,128)}, u32[]{:S(2)}) %copy-start) | copy-done | bytes 2097176
  1.6 0.0 copy-start.1
  1.6 0.9 %copy-done.1 = f32[128,256]{1,0:T(8,128)S(1)} copy-done((f32[128,256]{1,0:T(8,128)S(1)}, f32[128,256]{1,0:T(8,128)}, u32[]{:S(2)}) %copy-start.1) | copy-done | bytes 131096
  2.5 0.0 copy-start.2
  2.5 0.7 copy-done.2
  3.2 0.0 copy-start.3
  3.2 0.7 copy-done.3
  3.9 0.0 copy-start.4
  3.9 0.7 copy-done.4
  4.6 84.2 %ladder.1 = f32[128,2048]{1,0:T(8,128)S(1)} custom-call(f32[128,256]{1,0:T(8,128)S(1)} %copy-done.1, f32[256,2048]{1,0:T(8,128)S(1)} %copy-done, s32[32,64]{1,0:T(8,128)S(1)} %copy-done.2, s32[4,32]{1,0:T(4,128)S(1)} %copy-done.4, s32[32,32]{1,0:T(8,128)S(1)} %copy-done.3), custom_call_target="tpu_custom_call" | custom-call | flops 6442450944 | bytes 3276800 | tf_op jit(solution)/shard_map/ladder/pallas_call | solution.py:255
  88.9 1.0 %copy.7 = f32[128,2048]{1,0:T(8,128)} copy(f32[128,2048]{1,0:T(8,128)S(1)} %ladder.1) | data formatting | bytes 2097152
Async XLA Ops:
  0.0 1.6 %copy-start = (f32[256,2048]{1,0:T(8,128)S(1)}, f32[256,2048]{1,0:T(8,128)}, u32[]{:S(2)}) copy-start(f32[256,2048]{1,0:T(8,128)} %int_ref.1) | copy-start | bytes 6291460
  1.6 0.9 %copy-start.1 = (f32[128,256]{1,0:T(8,128)S(1)}, f32[128,256]{1,0:T(8,128)}, u32[]{:S(2)}) copy-start(f32[128,256]{1,0:T(8,128)} %amp_ref.1) | copy-start | bytes 393220
  2.5 0.7 copy-start.2
  3.2 0.7 copy-start.3
  3.9 0.7 copy-start.4

commit v2 on v1

v2 whole, which is shorter than its diff:
```python
import jax
import jax.numpy as jnp
from jax import lax
from jax.experimental import pallas as pl
from jax.experimental.pallas import tpu as pltpu
from jax.sharding import PartitionSpec as P

TILE = 64
W = 256
HALF = 128
BACKLOG = 1
LAG = 2
EARLY = 4
OWN, NEAR_X, NEAR_Z, FAR = 0, 1, 2, 3
MESH = pl.DeviceIdType.MESH
F32 = jnp.float32
BF16 = jnp.bfloat16


def device(x, z_lo, core, z_hi, y):
    return (z_lo * 8 + x * 2 + core, z_hi * 4 + y)


def remote(src, dst, send_sem, recv_sem, target):
    return pltpu.make_async_remote_copy(
        src_ref=src, dst_ref=dst, send_sem=send_sem, recv_sem=recv_sem,
        device_id=target, device_id_type=MESH,
    )


def onehot(shape, dim, offset):
    tile = lax.div(lax.broadcasted_iota(jnp.int32, shape, dim), TILE) + offset
    return (tile == lax.broadcasted_iota(jnp.int32, shape, 1 - dim)).astype(BF16)


def mm(a, b):
    return jnp.dot(a, b, preferred_element_type=F32)


def split(value):
    high = value.astype(BF16)
    return high, (value - high.astype(F32)).astype(BF16)


def kernel(
    amp_hbm, int_hbm, amp_mask_hbm, int_mask_hbm, res_mask_hbm, out_ref,
    amp_in, int_in, amp_tiles, int_tiles, res_in,
    out_v, st, af, ah, al, bf, bh, bl, part, r1x, r1z, r2x, r2z, res_tiles, mask8,
    s_in, s_out, s0, q0, s1, q1, sf1, s2, q2, sf2, qf2,
    sb, rb, ss, rs, sf, rf, s1x, q1x, s1z, q1z, s2x, q2x, s2z, q2z,
):
    n = bf.shape[1]
    loads = [
        pltpu.make_async_copy(src, dst, s_in.at[i])
        for i, (src, dst) in enumerate((
            (amp_hbm, amp_in), (amp_mask_hbm, amp_tiles), (int_mask_hbm, int_tiles),
            (int_hbm, int_in), (res_mask_hbm, res_in),
        ))
    ]
    for load in loads:
        load.start()

    row, col = lax.axis_index("row"), lax.axis_index("col")
    core, x, z = lax.rem(row, 2), lax.rem(lax.div(row, 2), 4), lax.div(row, 8)
    y, h = lax.rem(col, 4), lax.div(col, 4)
    odd = lax.rem(x, 2)
    xa = x + 1 - 2 * odd
    xb = lax.rem(x + 3 + 2 * odd, 4)
    sib = device(x, z, 1 - core, h, y)
    dev_a = device(xa, z, core, h, y)
    dev_b = device(xb, z, core, h, y)
    dev_z = device(x, 1 - z, core, h, y)
    y_up, y_down = lax.rem(y + 1, 4), lax.rem(y + 3, 4)
    dev_y = (device(x, z, core, h, y_up), device(x, z, core, h, y_down))
    kk = 2 * odd + core
    kk_sib = 2 * odd + 1 - core
    kk_a = 2 * (1 - odd) + core
    kk_as = 2 * (1 - odd) + 1 - core

    def at(z_to, h_to):
        return device(x, z_to, core, lax.rem(h_to + 8, 4), y)

    def flag(condition):
        return condition.astype(jnp.int32)

    q = lax.div(x, 2)
    is_source = lax.rem(h, 2) == q
    z_to = lax.div(h, 2)
    offset = lax.rem(z + z_to, 2)
    targets = (
        at(z_to, h + 1 - offset),
        at(z_to, h - (1 - offset) + offset * (1 - 2 * z_to)),
    )
    h_from = 2 * z + q
    place = lax.rem(h - h_from + 4, 4)
    home = place == 0
    relay = 3 - 2 * q
    side = 1 + 2 * z
    relays = (place == relay, jnp.logical_or(home, place == side))
    relay_to = (at(z, h_from + 2), at(z, h_from + 2 + flag(home) * (1 - 2 * z)))
    opposite = place == 2
    from_aligned = at(z, h_from + relay * flag(opposite))
    direct = flag(jnp.logical_or(home, place == side))
    from_offset = at(z + direct * (1 - 2 * z), h_from + side * flag(opposite))

    barrier = pltpu.get_barrier_semaphore()
    for peer in (sib, dev_a, dev_b, dev_z, *dev_y, from_offset):
        pl.semaphore_signal(barrier, inc=1, device_id=peer, device_id_type=MESH)

    @pl.when(jnp.logical_not(home))
    def _():
        pl.semaphore_signal(barrier, inc=1, device_id=from_aligned, device_id_type=MESH)

    for load in loads[:2]:
        load.wait()
    rows = mm(onehot((2 * TILE, 32), 0, 2 * row), amp_tiles[...].astype(BF16)).astype(BF16)
    st[0] = amp_in[...] * mm(rows, onehot((64, W), 1, 4 * col))

    def to_a(j):
        return remote(bf.at[kk, j], bf.at[kk, j], sb.at[j], rb.at[j], dev_a)

    def to_sib(j):
        return remote(bf.at[kk, j], bf.at[kk, j], ss.at[j], rs.at[j], sib)

    def forward(j):
        return remote(bf.at[kk_a, j], bf.at[kk_a, j], sf.at[j], rf.at[j], sib)

    for load in loads[2:4]:
        load.wait()
    mask8[...] = jnp.zeros_like(mask8)
    mask8[0:4, :] = int_tiles[...].astype(F32)
    mask8b = mask8[...].astype(BF16)

    def mask_int(j):
        tiles = mm(mask8b, onehot((32, W), 1, (W // TILE) * j))
        for t in range(4):
            r = slice(t * TILE, (t + 1) * TILE)
            bf[kk, j, r, :] = int_in[r, j * W:(j + 1) * W] * tiles[t:t + 1, :]

    for j in range(EARLY):
        mask_int(j)

    pl.semaphore_wait(barrier, 6 + 2 * flag(is_source) + flag(relays[0]) + flag(relays[1]))

    def half(p):
        return pl.ds(p * TILE, TILE)

    def leg0(p):
        return remote(st.at[0, half(p)], st.at[1, half(p)], s0.at[p], q0.at[p], dev_b)

    def leg1(b, i, p):
        s = 2 * offset + b
        return remote(
            st.at[b, half(p)], af.at[s, y, half(p)], s1.at[b, i, p], q1.at[s, p], targets[i]
        )

    def leg1_relay(s, p):
        block = af.at[s, y, half(p)]
        return remote(block, block, sf1.at[s, p], q1.at[s, p], relay_to[s // 2])

    def leg2(s, i, p):
        block = af.at[s, y, half(p)]
        return remote(block, block, s2.at[s, i, p], q2.at[s, i, p], dev_y[i])

    def leg2_landed(s, i, p):
        block = af.at[s, (y_down, y_up)[i], half(p)]
        return remote(block, block, s2.at[s, i, p], q2.at[s, i, p], dev_y[i])

    def leg2_relay(s, p):
        block = af.at[s, (y_down, y_up)[p], half(p)]
        return remote(block, block, sf2.at[s, p], qf2.at[s, p], dev_y[p])

    def leg2_relay_landed(s, p):
        block = af.at[s, lax.rem(y + 2, 4), half(p)]
        return remote(block, block, sf2.at[s, p], qf2.at[s, p], dev_y[p])

    aligned_source = jnp.logical_and(is_source, offset == 0)
    offset_source = jnp.logical_and(is_source, offset == 1)

    @pl.when(jnp.logical_not(is_source))
    def _():
        leg0(0).start()
        leg0(1).start()

    @pl.when(offset_source)
    def _():
        for p in range(2):
            leg1(0, 0, p).start()
            leg1(0, 1, p).start()

    @pl.when(home)
    def _():
        af[OWN, y] = st[0]

    for j in range(n):
        if j >= EARLY:
            mask_int(j)
        to_a(j).start()
        to_sib(j).start()

    @pl.when(is_source)
    def _():
        for p in range(2):
            leg0(p).wait_recv()
            leg1(1, 0, p).start()
            leg1(1, 1, p).start()

    @pl.when(home)
    def _():
        af[NEAR_X, y] = st[1]

    def spread_z(s):
        for p in range(2):
            def arrive():
                leg1_relay(s, p).wait_recv()

                @pl.when(relays[s // 2])
                def _():
                    leg1_relay(s, p).start()

            if s // 2:
                arrive()
            else:
                pl.when(jnp.logical_not(home))(arrive)
            leg2(s, 0, p).start()
            leg2(s, 1, p).start()

    def spread_y(s):
        for p in range(2):
            leg2_landed(s, p, p).wait_recv()
            leg2_relay(s, p).start()

    def take_amp(s):
        for p in range(2):
            leg2_landed(s, 1 - p, p).wait_recv()
            leg2_relay_landed(s, p).wait_recv()
        for k in range(4):
            c = slice(k * W, (k + 1) * W)
            ah[s, :, c], al[s, :, c] = split(af[s, k])

    loads[4].wait()
    res_rows = mm(onehot((2 * TILE, 32), 0, 2 * row), res_in[...].astype(BF16))
    res_tiles[...] = res_rows.astype(BF16)

    def take_int(j):
        remote(bf.at[kk_a, j], bf.at[kk_a, j], sb.at[j], rb.at[j], sib).wait_recv()
        forward(j).start()
        remote(bf.at[kk_sib, j], bf.at[kk_sib, j], ss.at[j], rs.at[j], sib).wait_recv()
        remote(bf.at[kk_as, j], bf.at[kk_as, j], sf.at[j], rf.at[j], sib).wait_recv()
        for q in range(4):
            r = slice(q * W, (q + 1) * W)
            bh[j, r, :], bl[j, r, :] = split(bf[q, j])

    def multiply(s, j):
        high = bh[j]
        total = mm(ah[s], high) + mm(al[s], high) + mm(ah[s], bl[j])
        part[s, j, 0] = total[:, :HALF]
        part[s, j, 1] = total[:, HALF:]

    def first_x(i, j):
        return remote(part.at[FAR - 2 * i, j, 0], r1x.at[j, i], s1x.at[j, i], q1x.at[j, i], dev_b)

    def first_z(i, j):
        return remote(part.at[FAR - i, j, 1], r1z.at[j, i], s1z.at[j, i], q1z.at[j, i], dev_z)

    def second_z(j):
        return remote(part.at[NEAR_Z, j, 0], r2z.at[j], s2z.at[j], q2z.at[j], dev_z)

    def second_x(j):
        return remote(part.at[NEAR_X, j, 1], r2x.at[j], s2x.at[j], q2x.at[j], dev_b)

    def far(j):
        multiply(FAR, j)
        first_x(0, j).start()
        first_z(0, j).start()

    def near_x(j):
        multiply(NEAR_X, j)
        first_x(1, j).start()

    def near_z(j):
        multiply(NEAR_Z, j)
        first_z(1, j).start()

    def second(j):
        first_x(0, j).wait_recv()
        part[NEAR_Z, j, 0] += r1x[j, 0]
        second_z(j).start()
        first_z(0, j).wait_recv()
        part[NEAR_X, j, 1] += r1z[j, 0]
        second_x(j).start()

    def loop(lo, hi, *steps):
        def body(j, carry):
            for step in steps:
                step(j)
            return carry

        lax.fori_loop(lo, hi, body, 0)

    def start_own():
        @pl.when(aligned_source)
        def _():
            for p in range(2):
                leg1(0, 0, p).start()
                leg1(0, 1, p).start()

    spread_z(NEAR_Z)
    spread_z(FAR)
    spread_y(NEAR_Z)
    spread_z(NEAR_X)
    spread_y(FAR)
    start_own()
    take_amp(NEAR_Z)
    loop(0, BACKLOG, take_int, near_z)
    spread_y(NEAR_X)
    take_amp(FAR)
    loop(0, BACKLOG, far)
    spread_z(OWN)
    take_amp(NEAR_X)
    loop(0, BACKLOG, near_x)
    loop(BACKLOG, LAG, take_int, far, near_z, near_x)
    loop(LAG, 5, take_int, far, near_z, near_x, lambda j: second(j - LAG))
    spread_y(OWN)
    loop(5, n, take_int, far, near_z, near_x, lambda j: second(j - LAG))
    take_amp(OWN)
    loop(0, n - LAG, lambda j: multiply(OWN, j))
    loop(n - LAG, n, second, lambda j: multiply(OWN, j))

    def store(j):
        c = pl.ds(pl.multiple_of(j * W, W), W)
        return pltpu.make_async_copy(out_v.at[:, c], out_ref.at[:, c], s_out.at[j])

    def finish(j):
        tiles = mm(res_tiles[...], onehot((32, W), 1, (W // TILE) * j))
        first_x(1, j).wait_recv()
        second_z(j).wait_recv()
        first_z(1, j).wait_recv()
        second_x(j).wait_recv()
        c = pl.multiple_of(j * W, W)
        left = part[OWN, j, 0] + r1x[j, 1] + r2z[j]
        right = part[OWN, j, 1] + r1z[j, 1] + r2x[j]
        out_v[:, pl.ds(c, HALF)] = left * tiles[:, :HALF]
        out_v[:, pl.ds(c + HALF, HALF)] = right * tiles[:, HALF:]
        store(j).start()

    loop(0, n, finish)

    @pl.when(jnp.logical_not(is_source))
    def _():
        leg0(0).wait_send()
        leg0(1).wait_send()

    @pl.when(is_source)
    def _():
        for b in range(2):
            for i in range(2):
                for p in range(2):
                    leg1(b, i, p).wait_send()

    for s in range(4):
        for p in range(2):
            @pl.when(relays[s // 2])
            def _():
                leg1_relay(s, p).wait_send()

            for i in range(2):
                leg2(s, i, p).wait_send()
            leg2_relay(s, p).wait_send()

    def drain(j):
        to_a(j).wait_send()
        to_sib(j).wait_send()
        forward(j).wait_send()
        for i in range(2):
            first_x(i, j).wait_send()
            first_z(i, j).wait_send()
        second_x(j).wait_send()
        second_z(j).wait_send()
        store(j).wait()

    loop(0, n, drain)


def on_device(amplitudes, integrals, amp_mask, int_mask, res_mask):
    rows, depth = amplitudes.shape
    cols = integrals.shape[1]
    n = cols // W
    dma = pltpu.SemaphoreType.DMA
    vmem = pltpu.VMEM
    return pl.pallas_call(
        kernel,
        out_shape=jax.ShapeDtypeStruct((rows, cols), F32),
        in_specs=[pl.BlockSpec(memory_space=pltpu.HBM)] * 5,
        out_specs=pl.BlockSpec(memory_space=pltpu.HBM),
        scratch_shapes=[
            vmem((rows, depth), F32),
            vmem((depth, cols), F32),
            vmem(amp_mask.shape, jnp.int32),
            vmem(int_mask.shape, jnp.int32),
            vmem(res_mask.shape, jnp.int32),
            vmem((rows, cols), F32),
            vmem((2, rows, depth), F32),
            vmem((4, 4, rows, depth), F32),
            vmem((4, rows, 4 * depth), BF16),
            vmem((4, rows, 4 * depth), BF16),
            vmem((4, n, depth, W), F32),
            vmem((n, 4 * depth, W), BF16),
            vmem((n, 4 * depth, W), BF16),
            vmem((4, n, 2, rows, HALF), F32),
            vmem((n, 2, rows, HALF), F32),
            vmem((n, 2, rows, HALF), F32),
            vmem((n, rows, HALF), F32),
            vmem((n, rows, HALF), F32),
            vmem((rows, 32), BF16),
            vmem((8, 32), F32),
            dma((5,)), dma((n,)), dma((2,)), dma((2,)), dma((2, 2, 2)), dma((4, 2)), dma((4, 2)),
            dma((4, 2, 2)), dma((4, 2, 2)), dma((4, 2)), dma((4, 2)),
            dma((n,)), dma((n,)), dma((n,)), dma((n,)), dma((n,)), dma((n,)),
            dma((n, 2)), dma((n, 2)), dma((n, 2)), dma((n, 2)),
            dma((n,)), dma((n,)), dma((n,)), dma((n,)),
        ],
        compiler_params=pltpu.CompilerParams(
            collective_id=0, has_side_effects=True, vmem_limit_bytes=60 * 2**20
        ),
        cost_estimate=pl.CostEstimate(
            flops=2 * 3 * 4 * rows * 4 * depth * cols,
            bytes_accessed=4 * (rows * depth + depth * cols + rows * cols),
            transcendentals=0,
        ),
        name="ladder",
    )(amplitudes, integrals, amp_mask, int_mask, res_mask)


def solution(mesh):
    placed = (P("row", "col"), P("row", "col"), P(), P("row", "col"), P(None, "col"))
    return jax.shard_map(
        on_device, mesh=mesh, in_specs=placed, out_specs=P("row", "col"), check_vma=False
    )
```

time: 90.1 us -> 76.4 us (0.85)
  Pallas kernels: 84.2 us -> 73.9 us
  local copies, waits for them, and re-layouts: 5.58 us -> 2.3 us
    pallas_call x1, Pallas kernels: 84.2 us -> 73.9 us  [on_device(): pl.pallas_call(kernel, out_shape=jax.ShapeDtypeStruct((rows, cols), F32),...]
    unnamed x11 -> x1, local copies, waits for them, and re-layouts: 5.58 us -> 2.3 us
where the time goes in v2:
time: 76.4 us; the launch traced here: 76.2 us
  Pallas kernels  73.9 us (97%)
  local copies, waits for them, and re-layouts  2.3 us (3%)
    pallas_call x1, Pallas kernels, on_device(): pl.pallas_call(kernel, out_shape=jax.ShapeDtypeStruct((rows, cols), F32),...  73.9 us
    unnamed x1, local copies, waits for them, and re-layouts  2.3 us

profile of v2, /device:TPU:1, one launch (start us, length us, event | category | flops | bytes accessed | tf_op | source)
XLA Modules:
  0.0 76.2 jit_solution(16205012104099542114)
XLA Ops:
  0.0 73.9 %ladder.1 = f32[128,2048]{1,0:T(8,128)} custom-call(f32[128,256]{1,0:T(8,128)} %amp_hbm.1, f32[256,2048]{1,0:T(8,128)} %int_hbm.1, s32[32,64]{1,0:T(8,128)} %amp_mask_hbm.1, s32[4,32]{1,0:T(4,128)} %int_mask_hbm.1, s32[32,32]{1,0:T(8,128)} %res_mask_hbm.1), custom_call_target="tpu_custom_call" | custom-call | flops 6442450944 | bytes 3276800 | tf_op jit(solution)/shard_map/ladder/pallas_call | solution.py:391
  73.9 2.3 %copy.7 = f32[128,2048]{1,0:T(8,128)} copy(f32[128,2048]{1,0:T(8,128)} %ladder.1) | data formatting | bytes 2097152

commit v3 on v2

--- a/solution.py
+++ b/solution.py
@@ -11,6 +11,8 @@
 BACKLOG = 1
 LAG = 2
 EARLY = 4
+PIECES = 2
+PIECE = 128 // PIECES
 OWN, NEAR_X, NEAR_Z, FAR = 0, 1, 2, 3
 MESH = pl.DeviceIdType.MESH
 F32 = jnp.float32
@@ -45,8 +47,8 @@
 def kernel(
     amp_hbm, int_hbm, amp_mask_hbm, int_mask_hbm, res_mask_hbm, out_ref,
     amp_in, int_in, amp_tiles, int_tiles, res_in,
-    out_v, st, af, ah, al, bf, bh, bl, part, r1x, r1z, r2x, r2z, res_tiles, mask8,
-    s_in, s_out, s0, q0, s1, q1, sf1, s2, q2, sf2, qf2,
+    st, af, ah, al, bf, bh, bl, part, r1x, r1z, r2x, r2z, res_tiles, mask8,
+    s_in, s0, q0, s1, q1, sf1, s2, q2, sf2, qf2,
     sb, rb, ss, rs, sf, rf, s1x, q1x, s1z, q1z, s2x, q2x, s2z, q2z,
 ):
     n = bf.shape[1]
@@ -142,49 +144,50 @@
 
     pl.semaphore_wait(barrier, 6 + 2 * flag(is_source) + flag(relays[0]) + flag(relays[1]))
 
-    def half(p):
-        return pl.ds(p * TILE, TILE)
+    def piece(p):
+        return pl.ds(p * PIECE, PIECE)
 
     def leg0(p):
-        return remote(st.at[0, half(p)], st.at[1, half(p)], s0.at[p], q0.at[p], dev_b)
+        return remote(st.at[0, piece(p)], st.at[1, piece(p)], s0.at[p], q0.at[p], dev_b)
 
     def leg1(b, i, p):
         s = 2 * offset + b
         return remote(
-            st.at[b, half(p)], af.at[s, y, half(p)], s1.at[b, i, p], q1.at[s, p], targets[i]
+            st.at[b, piece(p)], af.at[s, y, piece(p)], s1.at[b, i, p], q1.at[s, p], targets[i]
         )
 
     def leg1_relay(s, p):
-        block = af.at[s, y, half(p)]
+        block = af.at[s, y, piece(p)]
         return remote(block, block, sf1.at[s, p], q1.at[s, p], relay_to[s // 2])
 
     def leg2(s, i, p):
-        block = af.at[s, y, half(p)]
+        block = af.at[s, y, piece(p)]
         return remote(block, block, s2.at[s, i, p], q2.at[s, i, p], dev_y[i])
 
     def leg2_landed(s, i, p):
-        block = af.at[s, (y_down, y_up)[i], half(p)]
+        block = af.at[s, (y_down, y_up)[i], piece(p)]
         return remote(block, block, s2.at[s, i, p], q2.at[s, i, p], dev_y[i])
 
     def leg2_relay(s, p):
-        block = af.at[s, (y_down, y_up)[p], half(p)]
-        return remote(block, block, sf2.at[s, p], qf2.at[s, p], dev_y[p])
+        way = p // (PIECES // 2)
+        block = af.at[s, (y_down, y_up)[way], piece(p)]
+        return remote(block, block, sf2.at[s, p], qf2.at[s, p], dev_y[way])
 
     def leg2_relay_landed(s, p):
-        block = af.at[s, lax.rem(y + 2, 4), half(p)]
-        return remote(block, block, sf2.at[s, p], qf2.at[s, p], dev_y[p])
+        block = af.at[s, lax.rem(y + 2, 4), piece(p)]
+        return remote(block, block, sf2.at[s, p], qf2.at[s, p], dev_y[p // (PIECES // 2)])
 
     aligned_source = jnp.logical_and(is_source, offset == 0)
     offset_source = jnp.logical_and(is_source, offset == 1)
 
     @pl.when(jnp.logical_not(is_source))
     def _():
-        leg0(0).start()
-        leg0(1).start()
+        for p in range(PIECES):
+            leg0(p).start()
 
     @pl.when(offset_source)
     def _():
-        for p in range(2):
+        for p in range(PIECES):
             leg1(0, 0, p).start()
             leg1(0, 1, p).start()
 
@@ -200,7 +203,7 @@
 
     @pl.when(is_source)
     def _():
-        for p in range(2):
+        for p in range(PIECES):
             leg0(p).wait_recv()
             leg1(1, 0, p).start()
             leg1(1, 1, p).start()
@@ -210,7 +213,7 @@
         af[NEAR_X, y] = st[1]
 
     def spread_z(s):
-        for p in range(2):
+        for p in range(PIECES):
             def arrive():
                 leg1_relay(s, p).wait_recv()
 
@@ -226,13 +229,13 @@
             leg2(s, 1, p).start()
 
     def spread_y(s):
-        for p in range(2):
-            leg2_landed(s, p, p).wait_recv()
+        for p in range(PIECES):
+            leg2_landed(s, p // (PIECES // 2), p).wait_recv()
             leg2_relay(s, p).start()
 
     def take_amp(s):
-        for p in range(2):
-            leg2_landed(s, 1 - p, p).wait_recv()
+        for p in range(PIECES):
+            leg2_landed(s, 1 - p // (PIECES // 2), p).wait_recv()
             leg2_relay_landed(s, p).wait_recv()
         for k in range(4):
             c = slice(k * W, (k + 1) * W)
@@ -301,7 +304,7 @@
     def start_own():
         @pl.when(aligned_source)
         def _():
-            for p in range(2):
+            for p in range(PIECES):
                 leg1(0, 0, p).start()
                 leg1(0, 1, p).start()
 
@@ -327,10 +330,6 @@
     loop(0, n - LAG, lambda j: multiply(OWN, j))
     loop(n - LAG, n, second, lambda j: multiply(OWN, j))
 
-    def store(j):
-        c = pl.ds(pl.multiple_of(j * W, W), W)
-        return pltpu.make_async_copy(out_v.at[:, c], out_ref.at[:, c], s_out.at[j])
-
     def finish(j):
         tiles = mm(res_tiles[...], onehot((32, W), 1, (W // TILE) * j))
         first_x(1, j).wait_recv()
@@ -340,26 +339,25 @@
         c = pl.multiple_of(j * W, W)
         left = part[OWN, j, 0] + r1x[j, 1] + r2z[j]
         right = part[OWN, j, 1] + r1z[j, 1] + r2x[j]
-        out_v[:, pl.ds(c, HALF)] = left * tiles[:, :HALF]
-        out_v[:, pl.ds(c + HALF, HALF)] = right * tiles[:, HALF:]
-        store(j).start()
+        out_ref[:, pl.ds(c, HALF)] = left * tiles[:, :HALF]
+        out_ref[:, pl.ds(c + HALF, HALF)] = right * tiles[:, HALF:]
 
     loop(0, n, finish)
 
     @pl.when(jnp.logical_not(is_source))
     def _():
-        leg0(0).wait_send()
-        leg0(1).wait_send()
+        for p in range(PIECES):
+            leg0(p).wait_send()
 
     @pl.when(is_source)
     def _():
         for b in range(2):
             for i in range(2):
-                for p in range(2):
+                for p in range(PIECES):
                     leg1(b, i, p).wait_send()
 
     for s in range(4):
-        for p in range(2):
+        for p in range(PIECES):
             @pl.when(relays[s // 2])
             def _():
                 leg1_relay(s, p).wait_send()
@@ -377,7 +375,6 @@
             first_z(i, j).wait_send()
         second_x(j).wait_send()
         second_z(j).wait_send()
-        store(j).wait()
 
     loop(0, n, drain)
 
@@ -390,16 +387,15 @@
     vmem = pltpu.VMEM
     return pl.pallas_call(
         kernel,
-        out_shape=jax.ShapeDtypeStruct((rows, cols), F32),
+        out_shape=pltpu.VMEM((rows, cols), F32),
         in_specs=[pl.BlockSpec(memory_space=pltpu.HBM)] * 5,
-        out_specs=pl.BlockSpec(memory_space=pltpu.HBM),
+        out_specs=pl.BlockSpec(memory_space=pltpu.VMEM),
         scratch_shapes=[
             vmem((rows, depth), F32),
             vmem((depth, cols), F32),
             vmem(amp_mask.shape, jnp.int32),
             vmem(int_mask.shape, jnp.int32),
             vmem(res_mask.shape, jnp.int32),
-            vmem((rows, cols), F32),
             vmem((2, rows, depth), F32),
             vmem((4, 4, rows, depth), F32),
             vmem((4, rows, 4 * depth), BF16),
@@ -414,14 +410,15 @@
             vmem((n, rows, HALF), F32),
             vmem((rows, 32), BF16),
             vmem((8, 32), F32),
-            dma((5,)), dma((n,)), dma((2,)), dma((2,)), dma((2, 2, 2)), dma((4, 2)), dma((4, 2)),
-            dma((4, 2, 2)), dma((4, 2, 2)), dma((4, 2)), dma((4, 2)),
+            dma((5,)), dma((PIECES,)), dma((PIECES,)),
+            dma((2, 2, PIECES)), dma((4, PIECES)), dma((4, PIECES)),
+            dma((4, 2, PIECES)), dma((4, 2, PIECES)), dma((4, PIECES)), dma((4, PIECES)),
             dma((n,)), dma((n,)), dma((n,)), dma((n,)), dma((n,)), dma((n,)),
             dma((n, 2)), dma((n, 2)), dma((n, 2)), dma((n, 2)),
             dma((n,)), dma((n,)), dma((n,)), dma((n,)),
         ],
         compiler_params=pltpu.CompilerParams(
-            collective_id=0, has_side_effects=True, vmem_limit_bytes=60 * 2**20
+            collective_id=0, has_side_effects=True, vmem_limit_bytes=56 * 2**20
         ),
         cost_estimate=pl.CostEstimate(
             flops=2 * 3 * 4 * rows * 4 * depth * cols,
@@ -429,7 +426,10 @@
             transcendentals=0,
         ),
         name="ladder",
-    )(amplitudes, integrals, amp_mask, int_mask, res_mask)
+    )(*(
+        pltpu.with_memory_space_constraint(a, pltpu.HBM)
+        for a in (amplitudes, integrals, amp_mask, int_mask, res_mask)
+    ))
 
 
 def solution(mesh):

time: 76.4 us -> 74.4 us (0.974)
  local copies, waits for them, and re-layouts: 2.3 us -> 0.97 us
    unnamed x1, local copies, waits for them, and re-layouts: 2.3 us -> 0.97 us
where the time goes in v3:
time: 74.4 us; the launch traced here: 74.3 us
  Pallas kernels  73.3 us (99%)
  local copies, waits for them, and re-layouts  0.97 us (1%)
    pallas_call x1, Pallas kernels, on_device(): pl.pallas_call(kernel, out_shape=pltpu.VMEM((rows, cols), F32), in_specs=...  73.3 us

profile of v3, /device:TPU:1, one launch (start us, length us, event | category | flops | bytes accessed | tf_op | source)
XLA Modules:
  0.0 74.3 jit_solution(1976192886318688019)
XLA Ops:
  0.0 73.3 %ladder.1 = f32[128,2048]{1,0:T(8,128)S(1)} custom-call(f32[128,256]{1,0:T(8,128)} %amp_hbm.1, f32[256,2048]{1,0:T(8,128)} %int_hbm.1, s32[32,64]{1,0:T(8,128)} %amp_mask_hbm.1, s32[4,32]{1,0:T(4,128)} %int_mask_hbm.1, s32[32,32]{1,0:T(8,128)} %res_mask_hbm.1), custom_call_target="tpu_custom_call" | custom-call | flops 6442450944 | bytes 3276800 | tf_op jit(solution)/shard_map/ladder/pallas_call | solution.py:388
  73.4 1.0 %copy.7 = f32[128,2048]{1,0:T(8,128)} copy(f32[128,2048]{1,0:T(8,128)S(1)} %ladder.1) | data formatting | bytes 2097152
